TPU v7x, 256 devices: a whole 4x4x8 slice. The times are simulated.
256 devices in a mesh: blk: 32 (over z, y_hi, core), grp: 8 (over y_lo, x).
Axes of the slice: x: 4, y: 4 (y_hi: 2, y_lo: 2; y = y_hi * 2 + y_lo), z: 8, core: 2. Of those that a mesh axis runs over, the one named last changes fastest.
Arguments:
- coeffs: bfloat16 [4096, 360, 128], P('blk', 'grp'), may hold values from -6 to 6
- vectors: float32 [4096, 16], P(('blk', 'grp')), may hold values from -6 to 6
Outputs:
- next_vectors: float32 [4096, 16], P(('blk', 'grp'))
All inputs are finite; a program needn't handle non-finite values.
Results may differ from a plain program's by a relative error of at most 0.0015.
The roundings to bfloat16 on the way count: a program that leaves them out, or rounds other values in their place, can miss the bound.
Values may be sent and summed in bfloat16 or wider, within the bound.
No kernel may reach another device: no remote copies, remote signals or barrier semaphores. Data moves between devices by JAX's collectives and lax.ppermute only.
A program may use at most 64 MiB of HBM per device.

v0:
```python
import math
import jax
import jax.numpy as jnp
from jax import lax
from jax.sharding import PartitionSpec as P

sharpness = 2.5
epsilon = 1e-06


def passed_along(block, axis, distance):
    devices = range(lax.axis_size(axis))
    route = [((i - distance) % len(devices), i) for i in devices]
    return lax.ppermute(block, axis, route)


def trig_rows(freq_local, group_size):
    total = freq_local * group_size
    row_ids = jnp.arange(2 * total, dtype=jnp.int32)
    within = row_ids % (2 * freq_local)
    freq = row_ids // (2 * freq_local) * freq_local + within % freq_local
    angles = jnp.arange(total, dtype=jnp.int32)
    phase = (freq[:, None] * angles[None, :] % total).astype(jnp.float32) * (2.0 * math.pi / total)
    cos_part = jnp.cos(phase).astype(jnp.bfloat16)
    sin_part = (-jnp.sin(phase)).astype(jnp.bfloat16)
    return jnp.where((within >= freq_local)[:, None], sin_part, cos_part)


def per_device(coeffs, vectors):
    block, freq_local, channels = coeffs.shape
    half_width = channels // 2
    group_size = lax.axis_size("grp")
    group_index = lax.axis_index("grp")
    own_rows = vectors.shape[0]
    angles = freq_local * group_size
    squares = jnp.einsum("ikc,ikc->i", coeffs, coeffs, preferred_element_type=jnp.float32)
    total_sq = lax.psum(squares, "grp")
    inv_norm = lax.rsqrt(total_sq / (angles * channels) + epsilon)
    unit_coef = (coeffs.astype(jnp.float32) * inv_norm[:, None, None]).astype(jnp.bfloat16)
    before_blk = passed_along(unit_coef, "blk", 1)
    after_blk = passed_along(unit_coef, "blk", -1)
    columns = jnp.concatenate([unit_coef, before_blk, after_blk], axis=0)
    swapped = jnp.concatenate([-columns[..., half_width:], columns[..., :half_width]], axis=-1)
    real_part = jnp.einsum("ikc,jkc->kij", unit_coef, columns, preferred_element_type=jnp.float32)
    imag_part = jnp.einsum("ikc,jkc->kij", unit_coef, swapped, preferred_element_type=jnp.float32)
    pair_terms = jnp.concatenate([real_part, imag_part], axis=0).astype(jnp.bfloat16)
    trig_table = trig_rows(freq_local, group_size)
    factor = sharpness / math.sqrt(angles * channels)
    corr = jnp.einsum(
        "frj,fm->rjm",
        lax.all_to_all(pair_terms, "grp", split_axis=1, concat_axis=0, tiled=True),
        trig_table,
        preferred_element_type=jnp.float32,
    )
    weights = jnp.mean(jnp.exp(factor * corr), axis=-1)
    col_ids = jnp.arange(weights.shape[1], dtype=jnp.int32)
    own_ids = group_index * own_rows + jnp.arange(own_rows, dtype=jnp.int32)
    weights = jnp.where(col_ids[None, :] == own_ids[:, None], jnp.zeros_like(weights), weights)
    row_degree = jnp.sum(weights, axis=-1)
    local_degree = jnp.sum(row_degree)
    degree_sum = lax.psum(local_degree, ("blk", "grp"))
    inv_root = lax.rsqrt(row_degree)
    scaled = vectors * inv_root[:, None]
    block_vec = lax.all_gather(scaled, "grp", axis=0, tiled=True)
    prev_vec = passed_along(block_vec, "blk", 1)
    next_vec = passed_along(block_vec, "blk", -1)
    neigh = jnp.concatenate([block_vec, prev_vec, next_vec], axis=0)
    product = jnp.dot(weights, neigh, precision=lax.Precision.HIGHEST)
    image = product * inv_root[:, None] * (3.0 * block)
    root_degree = jnp.sqrt(row_degree)
    local_proj = jnp.dot(root_degree, image, precision=lax.Precision.HIGHEST)
    projection = lax.psum(local_proj, ("blk", "grp"))
    deflated = image - root_degree[:, None] * (projection / degree_sum)[None, :]
    column_sq = lax.psum(jnp.sum(deflated * deflated, axis=0), ("blk", "grp"))
    total_rows = own_rows * group_size * lax.axis_size("blk")
    return deflated * lax.rsqrt(column_sq / total_rows + epsilon)[None, :]


def solution(mesh):
    placed = (P("blk", "grp", None), P(("blk", "grp"), None))
    return jax.shard_map(
        per_device, mesh=mesh, in_specs=placed, out_specs=P(("blk", "grp"), None), check_vma=False
    )
```

profile of v0, /device:TPU:1, one launch (start us, length us, event | category | flops | bytes accessed | tf_op | source)
XLA Modules:
  0.0 412.6 jit_solution(10428899602804066392)
XLA Ops:
  0.0 1.8 fusion.8
  1.8 16.8 %psum.28 = f32[128]{0:T(128)S(1)} all-reduce(f32[128]{0:T(128)S(1)} %fusion.8), channel_id=1, replica_groups=mesh['blk'=32,'grp'=8] {'grp'}, use_global_device_ids=true, to_apply=%region_0.0 | all-reduce | flops 128 | bytes 1024 | tf_op jit(solution)/shard_map/psum | solution.py:37
  18.5 1.9 multiply_convert_fusion
  20.4 7.0 %collective-permute-start = (bf16[128,45,128]{2,0,1:T(8,128)(2,1)S(1)}, bf16[128,45,128]{2,0,1:T(8,128)(2,1)S(1)}, u32[]{:S(2)}, u32[]{:S(2)}) collective-permute-start(bf16[128,45,128]{2,0,1:T(8,128)(2,1)S(1)} %multiply_convert_fusion), channel_id=1, source_target_pairs={{248,0},{0,8},{8,16},{16,24},{24,32},{32,40},{40,48},{48,56},{56,6... | collective-permute-start | bytes 4423688 | tf_op jit(solution)/shard_map/ppermute | solution.py:14
  27.5 0.0 collective-permute-start.1
  27.5 32.1 %collective-permute-done = bf16[128,45,128]{2,0,1:T(8,128)(2,1)S(1)} collective-permute-done((bf16[128,45,128]{2,0,1:T(8,128)(2,1)S(1)}, bf16[128,45,128]{2,0,1:T(8,128)(2,1)S(1)}, u32[]{:S(2)}, u32[]{:S(2)}) %collective-permute-start) | collective-permute-done | bytes 1474592 | tf_op jit(solution)/shard_map/ppermute | solution.py:14
  59.6 2.9 collective-permute-done.1
  62.5 0.0 copy-start
  62.5 1.1 copy-done
  63.6 0.7 pad_maximum_fusion.1
  64.3 3.2 slice_negate_fusion
  67.5 0.0 copy-start.1
  67.5 7.4 %fusion.9 = bf16[45,128,384]{2,1,0:T(8,128)(2,1)} fusion(bf16[128,45,128]{2,0,1:T(8,128)(2,1)S(1)} %multiply_convert_fusion, bf16[384,45,64]{2,0,1:T(8,128)(2,1)} %get-tuple-element.10, bf16[384,45,64]{2,0,1:T(8,128)(2,1)S(1)} %get-tuple-element.9), kind=kOutput, calls=%fused_computation.13 | convolution fusion | flops 577290240 | bytes 10321920 | tf_op jit(solution)/shard_map/ikc,jkc->kij/dot_general | solution.py:45
  74.9 0.0 copy-done.1
  74.9 3.8 convolution_convert_fusion
  78.7 8.0 %pad_maximum_fusion = bf16[90,128,384]{2,1,0:T(8,128)(2,1)} fusion(bf16[45,128,384]{2,1,0:T(8,128)(2,1)} %fusion.9, bf16[45,128,384]{2,1,0:T(8,128)(2,1)} %convolution_convert_fusion), kind=kLoop, calls=%fused_computation | loop fusion | flops 4423680 | bytes 17694720 | tf_op jit(solution)/shard_map/concatenate | solution.py:46
  86.7 12.5 %copy.18 = bf16[90,128,384]{2,0,1:T(8,128)(2,1)} copy(bf16[90,128,384]{2,1,0:T(8,128)(2,1)} %pad_maximum_fusion) | data formatting | bytes 17694720 | tf_op jit(solution)/shard_map/concatenate | solution.py:46
  99.2 5.3 %all-to-all-start = ((bf16[90,128,384]{2,0,1:T(8,128)(2,1)}), bf16[90,128,384]{2,0,1:T(8,128)(2,1)}, u32[]{:S(2)}, u32[]{:S(2)}) async-start(bf16[90,128,384]{2,0,1:T(8,128)(2,1)} %copy.18), calls=%async_computation | async-start | bytes 18874368 | tf_op jit(solution)/shard_map/all_to_all | solution.py:51
  104.5 91.0 %all-to-all-done = bf16[90,128,384]{2,0,1:T(8,128)(2,1)} async-done(((bf16[90,128,384]{2,0,1:T(8,128)(2,1)}), bf16[90,128,384]{2,0,1:T(8,128)(2,1)}, u32[]{:S(2)}, u32[]{:S(2)}) %all-to-all-start) | async-done | bytes 8847392 | tf_op jit(solution)/shard_map/all_to_all | solution.py:51
  195.6 10.7 %copy.20 = bf16[8,90,16,384]{3,2,1,0:T(8,128)(2,1)} copy(bf16[8,90,16,384]{3,1,2,0:T(8,128)(2,1)} %bitcast.4) | data formatting | bytes 17694720 | tf_op jit(solution)/shard_map/all_to_all | solution.py:51
  206.2 0.0 copy-start.2
  206.2 12.9 %exponential_reduce_fusion = f32[16,384]{1,0:T(8,128)S(1)} fusion(bf16[720,16,384]{2,1,0:T(8,128)(2,1)} %bitcast.18, s32[720]{0:T(1024)S(1)} %fusion.39, pred[720]{0:T(1024)(128)(4,1)S(1)} %fusion.44), kind=kOutput, calls=%fused_computation.3 | convolution fusion | flops 3192836608 | bytes 8875536 | tf_op jit(solution)/shard_map/frj,fm->rjm/dot_general | solution.py:49
  219.1 0.7 fusion.32
  219.8 0.0 copy-done.2
  219.8 0.1 broadcast_multiply_fusion
  219.9 21.8 %all_gather.3 = f32[128,16]{1,0:T(8,128)S(1)} all-gather(f32[16,16]{1,0:T(8,128)S(1)} %broadcast_multiply_fusion), channel_id=1, replica_groups=mesh['blk'=32,'grp'=8] {'grp'}, dimensions={0}, use_global_device_ids=true | all-gather | bytes 9216 | tf_op jit(solution)/shard_map/all_gather | solution.py:64
  241.7 9.5 %collective-permute-start.2 = (f32[128,16]{1,0:T(8,128)S(1)}, f32[128,16]{1,0:T(8,128)S(1)}, u32[]{:S(2)}, u32[]{:S(2)}) collective-permute-start(f32[128,16]{1,0:T(8,128)S(1)} %all_gather.3), channel_id=1, source_target_pairs={{248,0},{0,8},{8,16},{16,24},{24,32},{32,40},{40,48},{48,56},{56,6... | collective-permute-start | bytes 24584 | tf_op jit(solution)/shard_map/ppermute | solution.py:14
  251.1 0.0 collective-permute-start.3
  251.2 1.3 collective-permute-done.2
  252.5 3.8 collective-permute-done.3
  256.4 0.2 fusion.12
  256.6 0.1 convolution_bitcast_fusion
  256.8 81.0 %all-reduce = (f32[16]{0:T(128)S(1)}, f32[]{:T(128)}) all-reduce(f32[16]{0:T(128)S(1)} %convolution_bitcast_fusion, f32[]{:T(128)} %get-tuple-element.5), channel_id=1, replica_groups=mesh['blk'=32,'grp'=8] {'blk','grp'}, use_global_device_ids=true, to_apply=%region_3.4 | all-reduce | flops 17 | bytes 136 | tf_op jit(solution)/shard_map/psum | solution.py:72
  337.8 0.6 broadcast_divide_fusion
  338.5 0.1 multiply_reduce_fusion
  338.6 73.4 %psum.31 = f32[16]{0:T(128)S(1)} all-reduce(f32[16]{0:T(128)S(1)} %multiply_reduce_fusion), channel_id=1, replica_groups=mesh['blk'=32,'grp'=8] {'blk','grp'}, use_global_device_ids=true, to_apply=%region_7.8 | all-reduce | flops 16 | bytes 128 | tf_op jit(solution)/shard_map/psum | solution.py:74
  412.0 0.7 fusion.37
  (9 shorter events, 0.2 us)
Async XLA Ops:
  20.4 39.1 %collective-permute-start = (bf16[128,45,128]{2,0,1:T(8,128)(2,1)S(1)}, bf16[128,45,128]{2,0,1:T(8,128)(2,1)S(1)}, u32[]{:S(2)}, u32[]{:S(2)}) collective-permute-start(bf16[128,45,128]{2,0,1:T(8,128)(2,1)S(1)} %multiply_convert_fusion), channel_id=1, source_target_pairs={{248,0},{0,8},{8,16},{16,24},{24,32},{32,40},{40,48},{48,56},{56,6... | collective-permute-start | bytes 4423688 | tf_op jit(solution)/shard_map/ppermute | solution.py:14
  27.5 35.0 %collective-permute-start.1 = (bf16[128,45,128]{2,0,1:T(8,128)(2,1)S(1)}, bf16[128,45,128]{2,0,1:T(8,128)(2,1)S(1)}, u32[]{:S(2)}, u32[]{:S(2)}) collective-permute-start(bf16[128,45,128]{2,0,1:T(8,128)(2,1)S(1)} %multiply_convert_fusion), channel_id=1, source_target_pairs={{8,0},{16,8},{24,16},{32,24},{40,32},{48,40},{56,48},{64,56},{72,6... | collective-permute-start | bytes 4423688 | tf_op jit(solution)/shard_map/ppermute | solution.py:14
  62.5 1.1 copy-start
  67.5 7.4 %copy-start.1 = (bf16[128,45,128]{2,0,1:T(8,128)(2,1)S(1)}, bf16[128,45,128]{2,0,1:T(8,128)(2,1)}, u32[]{:S(2)}) copy-start(bf16[128,45,128]{2,0,1:T(8,128)(2,1)} %copy-done) | copy-start | bytes 4423684
  99.2 96.4 %all-to-all-start = ((bf16[90,128,384]{2,0,1:T(8,128)(2,1)}), bf16[90,128,384]{2,0,1:T(8,128)(2,1)}, u32[]{:S(2)}, u32[]{:S(2)}) async-start(bf16[90,128,384]{2,0,1:T(8,128)(2,1)} %copy.18), calls=%async_computation | async-start | bytes 18874368 | tf_op jit(solution)/shard_map/all_to_all | solution.py:51
  206.2 13.6 %copy-start.2 = (f32[16,16]{1,0:T(8,128)S(1)}, f32[16,16]{1,0:T(8,128)}, u32[]{:S(2)}) copy-start(f32[16,16]{1,0:T(8,128)} %param.3) | copy-start | bytes 3076
  241.7 10.8 %collective-permute-start.2 = (f32[128,16]{1,0:T(8,128)S(1)}, f32[128,16]{1,0:T(8,128)S(1)}, u32[]{:S(2)}, u32[]{:S(2)}) collective-permute-start(f32[128,16]{1,0:T(8,128)S(1)} %all_gather.3), channel_id=1, source_target_pairs={{248,0},{0,8},{8,16},{16,24},{24,32},{32,40},{40,48},{48,56},{56,6... | collective-permute-start | bytes 24584 | tf_op jit(solution)/shard_map/ppermute | solution.py:14
  251.1 5.2 %collective-permute-start.3 = (f32[128,16]{1,0:T(8,128)S(1)}, f32[128,16]{1,0:T(8,128)S(1)}, u32[]{:S(2)}, u32[]{:S(2)}) collective-permute-start(f32[128,16]{1,0:T(8,128)S(1)} %all_gather.3), channel_id=1, source_target_pairs={{8,0},{16,8},{24,16},{32,24},{40,32},{48,40},{56,48},{64,56},{72,6... | collective-permute-start | bytes 24584 | tf_op jit(solution)/shard_map/ppermute | solution.py:14
where the time goes:
time: 413 us
  blocking collectives  193 us (47%)
  waiting for transfers between devices  131 us (32%)
  matrix products  24.5 us (6%)
  local copies, waits for them, and re-layouts  24.4 us (6%)
  starting transfers between devices  21.8 us (5%)
  other arithmetic  17.7 us (4%)
    all_to_all x1, waiting for transfers between devices, per_device(): lax.all_to_all(pair_terms, 'grp', split_axis=1, concat_axis=0, tiled=True)  91 us
    psum x1, blocking collectives, per_device(): projection = lax.psum(local_proj, ('blk', 'grp'))  81 us
    psum x1, blocking collectives, per_device(): column_sq = lax.psum(jnp.sum(deflated * deflated, axis=0), ('blk', 'grp'))  73.4 us
    ppermute x4, waiting for transfers between devices, passed_along(): return lax.ppermute(block, axis, route)  40.1 us
    all_gather x1, blocking collectives, per_device(): block_vec = lax.all_gather(scaled, 'grp', axis=0, tiled=True)  21.8 us
    psum x1, blocking collectives, per_device(): total_sq = lax.psum(squares, 'grp')  16.8 us
    ppermute x4, starting transfers between devices, passed_along(): return lax.ppermute(block, axis, route)  16.5 us
    dot_general x1, matrix products, per_device(): jnp.einsum('frj,fm->rjm', lax.all_to_all(pair_terms, 'grp', split_axis=1,...  12.9 us
  transfers between devices with their start and end apart: 5, of which 5 were waited for; matrix products, arithmetic and copies ran while one was open for 0% of the time, Pallas kernels for 0%

commit v1 on v0

--- a/solution.py
+++ b/solution.py
@@ -69,7 +69,7 @@
     image = product * inv_root[:, None] * (3.0 * block)
     root_degree = jnp.sqrt(row_degree)
     local_proj = jnp.dot(root_degree, image, precision=lax.Precision.HIGHEST)
-    projection = lax.psum(local_proj, ("blk", "grp"))
+    projection = lax.psum(lax.psum(local_proj, "grp"), "blk")
     deflated = image - root_degree[:, None] * (projection / degree_sum)[None, :]
     column_sq = lax.psum(jnp.sum(deflated * deflated, axis=0), ("blk", "grp"))
     total_rows = own_rows * group_size * lax.axis_size("blk")

time: 413 us -> 491 us (1.19)
  blocking collectives: 193 us -> 276 us
  waiting for transfers between devices: 131 us -> 126 us
    psum x1 -> x3, blocking collectives: 81 us -> 164 us  [the longest x2 82.4 us: per_device(): projection = lax.psum(lax.psum(local_proj, 'grp'), 'blk')]
    ppermute x4, waiting for transfers between devices: 40.1 us -> 35 us  [passed_along(): return lax.ppermute(block, axis, route)]
  transfers between devices with their start and end apart: 5 -> 5, of which waited for: 5 -> 3; matrix products, arithmetic and copies ran while one was open for 0% -> 0% of each run, Pallas kernels for 0% -> 0%
where the time goes in v1:
time: 491 us; the launch traced here: 490 us
  blocking collectives  276 us (56%)
  waiting for transfers between devices  126 us (26%)
  local copies, waits for them, and re-layouts  24.5 us (5%)
  matrix products  24.5 us (5%)
  starting transfers between devices  21.8 us (4%)
  other arithmetic  17.7 us (4%)
    all_to_all x1, waiting for transfers between devices, per_device(): lax.all_to_all(pair_terms, 'grp', split_axis=1, concat_axis=0, tiled=True)  91 us
    psum x2, blocking collectives, per_device(): projection = lax.psum(lax.psum(local_proj, 'grp'), 'blk')  82.4 us
    psum x1, blocking collectives, per_device(): degree_sum = lax.psum(local_degree, ('blk', 'grp'))  81.6 us
    psum x1, blocking collectives, per_device(): column_sq = lax.psum(jnp.sum(deflated * deflated, axis=0), ('blk', 'grp'))  73.3 us
    ppermute x4, waiting for transfers between devices, passed_along(): return lax.ppermute(block, axis, route)  35 us
    all_gather x1, blocking collectives, per_device(): block_vec = lax.all_gather(scaled, 'grp', axis=0, tiled=True)  21.8 us
    psum x1, blocking collectives, per_device(): total_sq = lax.psum(squares, 'grp')  16.8 us
    ppermute x4, starting transfers between devices, passed_along(): return lax.ppermute(block, axis, route)  16.5 us
  transfers between devices with their start and end apart: 5, of which 3 were waited for; matrix products, arithmetic and copies ran while one was open for 0% of the time, Pallas kernels for 0%

profile of v1, /device:TPU:1, one launch (start us, length us, event | category | flops | bytes accessed | tf_op | source)
XLA Modules:
  0.0 490.4 jit_solution(13283157307604562460)
XLA Ops:
  0.0 1.8 fusion.8
  1.8 16.8 %psum.35 = f32[128]{0:T(128)S(1)} all-reduce(f32[128]{0:T(128)S(1)} %fusion.8), channel_id=1, replica_groups=mesh['blk'=32,'grp'=8] {'grp'}, use_global_device_ids=true, to_apply=%region_0.0 | all-reduce | flops 128 | bytes 1024 | tf_op jit(solution)/shard_map/psum | solution.py:37
  18.5 1.9 multiply_convert_fusion
  20.4 7.0 %collective-permute-start = (bf16[128,45,128]{2,0,1:T(8,128)(2,1)S(1)}, bf16[128,45,128]{2,0,1:T(8,128)(2,1)S(1)}, u32[]{:S(2)}, u32[]{:S(2)}) collective-permute-start(bf16[128,45,128]{2,0,1:T(8,128)(2,1)S(1)} %multiply_convert_fusion), channel_id=1, source_target_pairs={{248,0},{0,8},{8,16},{16,24},{24,32},{32,40},{40,48},{48,56},{56,6... | collective-permute-start | bytes 4423688 | tf_op jit(solution)/shard_map/ppermute | solution.py:14
  27.5 0.0 collective-permute-start.1
  27.5 32.1 %collective-permute-done = bf16[128,45,128]{2,0,1:T(8,128)(2,1)S(1)} collective-permute-done((bf16[128,45,128]{2,0,1:T(8,128)(2,1)S(1)}, bf16[128,45,128]{2,0,1:T(8,128)(2,1)S(1)}, u32[]{:S(2)}, u32[]{:S(2)}) %collective-permute-start) | collective-permute-done | bytes 1474592 | tf_op jit(solution)/shard_map/ppermute | solution.py:14
  59.6 2.9 collective-permute-done.1
  62.5 0.0 copy-start
  62.5 1.1 copy-done
  63.6 0.7 pad_maximum_fusion.1
  64.3 3.2 slice_negate_fusion
  67.5 0.0 copy-start.1
  67.5 7.4 %fusion.9 = bf16[45,128,384]{2,1,0:T(8,128)(2,1)} fusion(bf16[128,45,128]{2,0,1:T(8,128)(2,1)S(1)} %multiply_convert_fusion, bf16[384,45,64]{2,0,1:T(8,128)(2,1)} %get-tuple-element.8, bf16[384,45,64]{2,0,1:T(8,128)(2,1)S(1)} %get-tuple-element.7), kind=kOutput, calls=%fused_computation.13 | convolution fusion | flops 577290240 | bytes 10321920 | tf_op jit(solution)/shard_map/ikc,jkc->kij/dot_general | solution.py:45
  74.9 0.0 copy-done.1
  74.9 3.8 convolution_convert_fusion
  78.7 8.0 %pad_maximum_fusion = bf16[90,128,384]{2,1,0:T(8,128)(2,1)} fusion(bf16[45,128,384]{2,1,0:T(8,128)(2,1)} %fusion.9, bf16[45,128,384]{2,1,0:T(8,128)(2,1)} %convolution_convert_fusion), kind=kLoop, calls=%fused_computation | loop fusion | flops 4423680 | bytes 17694720 | tf_op jit(solution)/shard_map/concatenate | solution.py:46
  86.7 12.5 %copy.18 = bf16[90,128,384]{2,0,1:T(8,128)(2,1)} copy(bf16[90,128,384]{2,1,0:T(8,128)(2,1)} %pad_maximum_fusion) | data formatting | bytes 17694720 | tf_op jit(solution)/shard_map/concatenate | solution.py:46
  99.2 5.3 %all-to-all-start = ((bf16[90,128,384]{2,0,1:T(8,128)(2,1)}), bf16[90,128,384]{2,0,1:T(8,128)(2,1)}, u32[]{:S(2)}, u32[]{:S(2)}) async-start(bf16[90,128,384]{2,0,1:T(8,128)(2,1)} %copy.18), calls=%async_computation | async-start | bytes 18874368 | tf_op jit(solution)/shard_map/all_to_all | solution.py:51
  104.5 91.0 %all-to-all-done = bf16[90,128,384]{2,0,1:T(8,128)(2,1)} async-done(((bf16[90,128,384]{2,0,1:T(8,128)(2,1)}), bf16[90,128,384]{2,0,1:T(8,128)(2,1)}, u32[]{:S(2)}, u32[]{:S(2)}) %all-to-all-start) | async-done | bytes 8847392 | tf_op jit(solution)/shard_map/all_to_all | solution.py:51
  195.6 10.7 %copy.20 = bf16[8,90,16,384]{3,2,1,0:T(8,128)(2,1)} copy(bf16[8,90,16,384]{3,1,2,0:T(8,128)(2,1)} %bitcast.4) | data formatting | bytes 17694720 | tf_op jit(solution)/shard_map/all_to_all | solution.py:51
  206.2 0.0 copy-start.2
  206.2 12.9 %exponential_reduce_fusion = f32[16,384]{1,0:T(8,128)S(1)} fusion(bf16[720,16,384]{2,1,0:T(8,128)(2,1)} %bitcast.18, s32[720]{0:T(1024)S(1)} %fusion.39, pred[720]{0:T(1024)(128)(4,1)S(1)} %fusion.44), kind=kOutput, calls=%fused_computation.3 | convolution fusion | flops 3192836608 | bytes 8875536 | tf_op jit(solution)/shard_map/frj,fm->rjm/dot_general | solution.py:49
  219.1 0.7 fusion.32
  219.8 0.0 copy-done.2
  219.8 0.1 broadcast_multiply_fusion
  219.9 21.8 %all_gather.3 = f32[128,16]{1,0:T(8,128)S(1)} all-gather(f32[16,16]{1,0:T(8,128)S(1)} %broadcast_multiply_fusion), channel_id=1, replica_groups=mesh['blk'=32,'grp'=8] {'grp'}, dimensions={0}, use_global_device_ids=true | all-gather | bytes 9216 | tf_op jit(solution)/shard_map/all_gather | solution.py:64
  241.7 9.5 %collective-permute-start.2 = (f32[128,16]{1,0:T(8,128)S(1)}, f32[128,16]{1,0:T(8,128)S(1)}, u32[]{:S(2)}, u32[]{:S(2)}) collective-permute-start(f32[128,16]{1,0:T(8,128)S(1)} %all_gather.3), channel_id=1, source_target_pairs={{248,0},{0,8},{8,16},{16,24},{24,32},{32,40},{40,48},{48,56},{56,6... | collective-permute-start | bytes 24584 | tf_op jit(solution)/shard_map/ppermute | solution.py:14
  251.1 0.0 collective-permute-start.3
  251.1 81.6 %psum.38 = f32[]{:T(128)} all-reduce(f32[]{:T(128)} %get-tuple-element.5), channel_id=1, replica_groups=mesh['blk'=32,'grp'=8] {'blk','grp'}, use_global_device_ids=true, to_apply=%region_6.7 | all-reduce | flops 1 | bytes 8 | tf_op jit(solution)/shard_map/psum | solution.py:61
  332.8 0.0 collective-permute-done.2
  332.8 0.1 copy.23
  332.8 0.0 collective-permute-done.3
  332.8 0.1 copy.24
  332.9 0.2 fusion.12
  333.2 0.1 convolution_bitcast_fusion
  333.3 13.7 %psum.36 = f32[16]{0:T(128)S(1)} all-reduce(f32[16]{0:T(128)S(1)} %convolution_bitcast_fusion), channel_id=1, replica_groups=mesh['blk'=32,'grp'=8] {'grp'}, use_global_device_ids=true, to_apply=%region_3.4 | all-reduce | flops 16 | bytes 128 | tf_op jit(solution)/shard_map/psum | solution.py:72
  347.0 68.7 %psum.37 = f32[16]{0:T(128)S(1)} all-reduce(f32[16]{0:T(128)S(1)} %psum.36), channel_id=1, replica_groups=mesh['blk'=32,'grp'=8] {'blk'}, use_global_device_ids=true, to_apply=%region_4.5 | all-reduce | flops 16 | bytes 128 | tf_op jit(solution)/shard_map/psum | solution.py:72
  415.7 0.6 broadcast_divide_fusion
  416.4 0.1 multiply_reduce_fusion
  416.4 73.3 %psum.39 = f32[16]{0:T(128)S(1)} all-reduce(f32[16]{0:T(128)S(1)} %multiply_reduce_fusion), channel_id=1, replica_groups=mesh['blk'=32,'grp'=8] {'blk','grp'}, use_global_device_ids=true, to_apply=%region_8.9 | all-reduce | flops 16 | bytes 128 | tf_op jit(solution)/shard_map/psum | solution.py:74
  489.7 0.7 fusion.37
  (7 shorter events, 0.1 us)
Async XLA Ops:
  20.4 39.1 %collective-permute-start = (bf16[128,45,128]{2,0,1:T(8,128)(2,1)S(1)}, bf16[128,45,128]{2,0,1:T(8,128)(2,1)S(1)}, u32[]{:S(2)}, u32[]{:S(2)}) collective-permute-start(bf16[128,45,128]{2,0,1:T(8,128)(2,1)S(1)} %multiply_convert_fusion), channel_id=1, source_target_pairs={{248,0},{0,8},{8,16},{16,24},{24,32},{32,40},{40,48},{48,56},{56,6... | collective-permute-start | bytes 4423688 | tf_op jit(solution)/shard_map/ppermute | solution.py:14
  27.5 35.0 %collective-permute-start.1 = (bf16[128,45,128]{2,0,1:T(8,128)(2,1)S(1)}, bf16[128,45,128]{2,0,1:T(8,128)(2,1)S(1)}, u32[]{:S(2)}, u32[]{:S(2)}) collective-permute-start(bf16[128,45,128]{2,0,1:T(8,128)(2,1)S(1)} %multiply_convert_fusion), channel_id=1, source_target_pairs={{8,0},{16,8},{24,16},{32,24},{40,32},{48,40},{56,48},{64,56},{72,6... | collective-permute-start | bytes 4423688 | tf_op jit(solution)/shard_map/ppermute | solution.py:14
  62.5 1.1 copy-start
  67.5 7.4 %copy-start.1 = (bf16[128,45,128]{2,0,1:T(8,128)(2,1)S(1)}, bf16[128,45,128]{2,0,1:T(8,128)(2,1)}, u32[]{:S(2)}) copy-start(bf16[128,45,128]{2,0,1:T(8,128)(2,1)} %copy-done) | copy-start | bytes 4423684
  99.2 96.4 %all-to-all-start = ((bf16[90,128,384]{2,0,1:T(8,128)(2,1)}), bf16[90,128,384]{2,0,1:T(8,128)(2,1)}, u32[]{:S(2)}, u32[]{:S(2)}) async-start(bf16[90,128,384]{2,0,1:T(8,128)(2,1)} %copy.18), calls=%async_computation | async-start | bytes 18874368 | tf_op jit(solution)/shard_map/all_to_all | solution.py:51
  206.2 13.6 %copy-start.2 = (f32[16,16]{1,0:T(8,128)S(1)}, f32[16,16]{1,0:T(8,128)}, u32[]{:S(2)}) copy-start(f32[16,16]{1,0:T(8,128)} %param.3) | copy-start | bytes 3076
  241.7 91.1 %collective-permute-start.2 = (f32[128,16]{1,0:T(8,128)S(1)}, f32[128,16]{1,0:T(8,128)S(1)}, u32[]{:S(2)}, u32[]{:S(2)}) collective-permute-start(f32[128,16]{1,0:T(8,128)S(1)} %all_gather.3), channel_id=1, source_target_pairs={{248,0},{0,8},{8,16},{16,24},{24,32},{32,40},{40,48},{48,56},{56,6... | collective-permute-start | bytes 24584 | tf_op jit(solution)/shard_map/ppermute | solution.py:14
  251.1 81.7 %collective-permute-start.3 = (f32[128,16]{1,0:T(8,128)S(1)}, f32[128,16]{1,0:T(8,128)S(1)}, u32[]{:S(2)}, u32[]{:S(2)}) collective-permute-start(f32[128,16]{1,0:T(8,128)S(1)} %all_gather.3), channel_id=1, source_target_pairs={{8,0},{16,8},{24,16},{32,24},{40,32},{48,40},{56,48},{64,56},{72,6... | collective-permute-start | bytes 24584 | tf_op jit(solution)/shard_map/ppermute | solution.py:14
